TPU v7x, 256 devices: a whole 4x4x8 slice. The times are simulated.
256 devices in a mesh: member: 8 (over x_lo, y), grid: 32 (over x_hi, z, core).
Axes of the slice: x: 4 (x_hi: 2, x_lo: 2; x = x_hi * 2 + x_lo), y: 4, z: 8, core: 2. Of those that a mesh axis runs over, the one named last changes fastest.
Arguments:
- latent: bfloat16 [8, 8192, 1024], P('member', 'grid'), may hold values from -6 to 6
- grid_latent_skip: bfloat16 [8, 16384, 1024], P('member', 'grid'), may hold values from -6 to 6
- initial_member_state: float32 [8, 100, 16384], P('member', None, 'grid'), may hold values from -6 to 6
- target: float32 [100, 16384], P(None, 'grid'), may hold values from -6 to 6
- neighbours: int32 [3, 16384], P(None, 'grid'), may hold values from 0 to 511, as said below
- edge_weight: float32 [3, 16384], P(None, 'grid'), may hold values from 0.2 to 1
- area_weight: float32 [16384], P('grid'), may hold values from 0.3 to 27, as said below
- variable_weight: float32 [100], replicated, may hold values from 0.3 to 3
- output_projection: bfloat16 [100, 1024], replicated, may hold values from -0.1875 to 0.1875
- layer_norm_gain: float32 [1024], replicated, may hold values from 0.1 to 1.9
Outputs:
- fair_crps: float32 [], replicated
- latent_grad: bfloat16 [8, 8192, 1024], P('member', 'grid')
- out_weight_grad: float32 [100, 1024], replicated
- norm_gain_grad: float32 [1024], replicated
Inputs may be any that keep to these rules, and one draw needn't show every extreme that they name: neighbours[k, p] indexes 256 + 2 * 128 rows ordered by latitude: the 128 last mesh rows of the slab below the point's slab, the slab's own 256 rows, then the 128 first rows of the slab above. `area_weight`: positive.
All inputs are finite; a program needn't handle non-finite values.
Results may differ from a plain program's by a relative error of at most 0.0067.
Values may be sent and summed in bfloat16 or wider, within the bound.
No kernel may reach another device: no remote copies, remote signals or barrier semaphores. Data moves between devices by JAX's collectives and lax.ppermute only.
A program may use at most 64 MiB of HBM per device.

v0:
```python
import jax
import jax.numpy as jnp
from jax import lax
from jax.sharding import PartitionSpec as P

SMOOTHING = 0.25
FAIRNESS = 0.95
norm_eps = 1e-05


def with_halo(array, sides, width):
    for axis, dim in sides:
        size, length = (lax.axis_size(axis), array.shape[dim])
        up = [(i, (i + 1) % size) for i in range(size - 1)]
        down = [(j, i) for i, j in up]
        last = lax.slice_in_dim(array, length - width, length, axis=dim)
        initial = lax.slice_in_dim(array, 0, width, axis=dim)
        before = lax.ppermute(last, axis, up)
        after = lax.ppermute(initial, axis, down)
        array = jnp.concatenate([before, array, after], axis=dim)
    return array


def from_behind(block, axis, distance):
    devices = range(lax.axis_size(axis))
    route = [(i - distance, i) for i in devices if i - distance in devices]
    return lax.ppermute(block, axis, route)


def smooth_abs(value):
    return jnp.sqrt(value * value + SMOOTHING * SMOOTHING)


def per_device(
    latent,
    grid_latent_skip,
    initial_member_state,
    target,
    neighbours,
    edge_weight,
    area_weight,
    variable_weight,
    output_projection,
    layer_norm_gain,
):
    mesh_count = latent.shape[1]
    rim = mesh_count // 2
    points = grid_latent_skip.shape[1]
    slots = neighbours.shape[0]
    variables = output_projection.shape[0]
    member_list = lax.axis_size("member")
    extended = with_halo(latent, (("grid", 1),), rim)[0]
    weight_arrays = edge_weight / jnp.sum(edge_weight, axis=0, keepdims=True)
    mixed = grid_latent_skip[0].astype(jnp.float32)
    for slot in range(slots):
        mixed = mixed + weight_arrays[slot][:, None] * jnp.take(
            extended, neighbours[slot], axis=0
        ).astype(jnp.float32)
    centred = mixed - jnp.mean(mixed, axis=1, keepdims=True)
    rscale = lax.rsqrt(jnp.mean(centred * centred, axis=1, keepdims=True) + norm_eps)
    normed = centred * rscale
    scaled = (normed * layer_norm_gain[None, :]).astype(jnp.bfloat16)
    predicted_field = initial_member_state[0] + lax.dot_general(
        output_projection, scaled, (((1,), (1,)), ((), ())), preferred_element_type=jnp.float32
    )
    weight_map = variable_weight[:, None] * area_weight[None, :]
    pair_distance = predicted_field - target
    spread = smooth_abs(pair_distance)
    eps_fair = (1.0 - FAIRNESS) / member_list
    coef_pair = (1.0 - eps_fair) / (member_list * (member_list - 1))
    every_member_set = lax.all_gather(predicted_field[None], "member", axis=0, tiled=True)
    member_difference = predicted_field[None] - every_member_set
    dist = smooth_abs(member_difference)
    pair_total = jnp.sum(dist, axis=0) - SMOOTHING
    pair_slope = jnp.sum(member_difference / dist, axis=0)
    pair_loss = jnp.sum(weight_map * pair_total)
    local_loss = jnp.sum(weight_map * spread) / member_list - 0.5 * coef_pair * pair_loss
    fore_grad = (
        weight_map * (pair_distance / spread / member_list - coef_pair * pair_slope)
    ).astype(jnp.bfloat16)
    wout_part = jnp.dot(fore_grad, scaled, preferred_element_type=jnp.float32)
    scaled_grad = lax.dot_general(
        fore_grad, output_projection, (((0,), (0,)), ((), ())), preferred_element_type=jnp.float32
    )
    gain_part = jnp.sum(scaled_grad * normed, axis=0)
    norm_grad = scaled_grad * layer_norm_gain[None, :]
    mixed_grad = rscale * (
        norm_grad
        - jnp.mean(norm_grad, axis=1, keepdims=True)
        - normed * jnp.mean(norm_grad * normed, axis=1, keepdims=True)
    )
    collect = jnp.zeros((extended.shape[0], extended.shape[1]), jnp.float32)
    for slot in range(slots):
        collect = collect.at[neighbours[slot]].add(weight_arrays[slot][:, None] * mixed_grad)
    from_above = from_behind(collect[:rim].astype(jnp.bfloat16), "grid", -1).astype(jnp.float32)
    from_below = from_behind(collect[rim + mesh_count :].astype(jnp.bfloat16), "grid", 1).astype(
        jnp.float32
    )
    owned = collect[rim : rim + mesh_count] + jnp.concatenate([from_below, from_above], axis=0)
    sums = lax.psum((wout_part, gain_part, local_loss), ("member", "grid"))
    fair_crps = sums[2] / (points * lax.axis_size("grid") * variables)
    return (fair_crps, owned[None].astype(jnp.bfloat16), sums[0], sums[1])


def solution(mesh):
    placed = (
        P("member", "grid", None),
        P("member", "grid", None),
        P("member", None, "grid"),
        P(None, "grid"),
        P(None, "grid"),
        P(None, "grid"),
        P("grid"),
        P(),
        P(),
        P(),
    )
    return jax.shard_map(
        per_device,
        mesh=mesh,
        in_specs=placed,
        out_specs=(P(), P("member", "grid", None), P(), P()),
        check_vma=False,
    )
```

profile of v0, /device:TPU:2, one launch (start us, length us, event | category | flops | bytes accessed | tf_op | source)
XLA Modules:
  0.0 378.3 jit_solution(10001090698908370508)
XLA Ops:
  7.2 0.0 copy-start
  7.2 0.0 all-gather.4.cloned.1.call-start
  7.2 1.1 fusion.24
  8.3 1.8 collective-permute-start
  10.1 1.3 collective-permute-start.1
  11.4 0.8 fusion.26
  12.3 0.7 reduce_sum.90
  13.0 0.7 broadcast_divide_fusion
  13.8 0.0 collective-permute-done
  13.8 1.5 collective-permute-done.1
  15.2 1.1 maximum_bitcast_fusion
  16.3 2.1 gather_fusion.2
  18.4 2.8 gather_fusion.1
  21.2 2.8 gather_fusion
  24.0 2.8 fusion.21
  26.8 0.0 copy-start.6
  26.8 0.3 multiply_reduce_fusion.2
  27.2 0.3 copy-done.6
  27.5 0.3 multiply_convert_fusion
  27.8 0.0 copy-done
  27.9 0.3 copy-done.4
  28.1 1.1 fusion.11
  29.3 0.0 all-gather.4.cloned.1.call-update
  29.3 0.0 all-reduce.3.cloned.1.call-start
  29.4 0.0 copy-done.7
  29.4 49.7 %all-gather.4.cloned.1.call-done = f32[8,100,512]{2,1,0:T(8,128)} async-done(((f32[1,100,512]{2,1,0:T(8,128)}), f32[8,100,512]{2,1,0:T(8,128)}) %all-gather.4.cloned.1.call-update) | async-done | bytes 1638416 | tf_op jit(solution)/shard_map/all_gather | solution.py:71
  79.0 2.5 fusion.10
  81.5 0.0 copy-done.8
  81.5 0.0 copy-done.9
  81.6 0.8 fusion.19
  82.4 0.9 multiply_reduce_fusion
  83.3 1.9 subtract_multiply_fusion
  85.2 7.4 %scatter_custom_fusion = f32[512,1024]{1,0:T(8,128)} fusion(s32[512]{0:T(512)S(1)} %bitcast.51, f32[512,1024]{1,0:T(8,128)} %subtract_multiply_fusion, f32[]{:T(128)} %constant.19.clone.1, f32[512]{0:T(512)S(1)} %bitcast.42), kind=kCustom, calls=%fused_computation.14 | custom fusion | flops 1048576 | bytes 4196356 | tf_op jit(solution)/shard_map/scatter-add | solution.py:94
  92.7 0.0 copy-done.1
  92.7 7.7 %scatter_custom_fusion.1 = f32[512,1024]{1,0:T(8,128)} fusion(f32[512,1024]{1,0:T(8,128)} %scatter_custom_fusion, s32[512]{0:T(512)S(1)} %bitcast.50, f32[512,1024]{1,0:T(8,128)S(1)} %copy-done.1, f32[512]{0:T(512)S(1)} %bitcast.40), kind=kCustom, calls=%fused_computation.12 | custom fusion | flops 1048576 | bytes 4196352 | tf_op jit(solution)/shard_map/scatter-add | solution.py:94
  100.4 7.7 %scatter_custom_fusion.2 = f32[512,1024]{1,0:T(8,128)} fusion(f32[512,1024]{1,0:T(8,128)} %scatter_custom_fusion.1, s32[512]{0:T(512)S(1)} %bitcast.49, f32[512,1024]{1,0:T(8,128)S(1)} %copy-done.1, f32[512]{0:T(512)S(1)} %bitcast.38), kind=kCustom, calls=%fused_computation.10 | custom fusion | flops 1048576 | bytes 4196352 | tf_op jit(solution)/shard_map/scatter-add | solution.py:94
  108.2 1.7 convert.6
  109.9 0.8 fusion.23
  110.8 2.0 collective-permute-start.2
  112.7 1.3 collective-permute-start.3
  114.0 1.1 fusion.27
  115.1 0.0 all-reduce.3.cloned.1.call-update
  116.4 79.3 %all-reduce = (f32[]{:T(128)}, f32[1024]{0:T(1024)}) all-reduce(f32[]{:T(128)S(6)} %sub.46, f32[1024]{0:T(1024)S(1)} %get-tuple-element.5), channel_id=1, replica_groups=mesh['member'=8,'grid'=32] {'member','grid'}, use_global_device_ids=true, to_apply=%region_6.8 | all-reduce | flops 1025 | bytes 8200 | tf_op jit(solution)/shard_map/psum | solution.py:100
  196.3 0.0 collective-permute-done.2
  196.3 0.0 collective-permute-done.3
  196.4 2.0 fusion.17
  198.3 170.2 %all-reduce.3.cloned.1.call-done = f32[100,1024]{1,0:T(8,128)} async-done(((f32[100,1024]{1,0:T(8,128)}), f32[100,1024]{1,0:T(8,128)}) %all-reduce.3.cloned.1.call-update) | async-done | bytes 409616 | tf_op jit(solution)/shard_map/psum | solution.py:100
  368.6 1.8 copy.19
  (25 shorter events, 0.1 us)
Async XLA Ops:
  7.2 20.7 %copy-start = (bf16[100,1024]{1,0:T(8,128)(2,1)S(1)}, bf16[100,1024]{1,0:T(8,128)(2,1)}, u32[]{:S(2)}) copy-start(bf16[100,1024]{1,0:T(8,128)(2,1)} %param.20) | copy-start | bytes 614404
  7.2 71.9 %all-gather.4.cloned.1.call-start = ((), (), s32[]{:S(2)}) async-start(), calls=%async_computation.1 | async-start | bytes 1916928 | tf_op jit(solution)/shard_map/all_gather | solution.py:71
  8.3 5.4 %collective-permute-start = (bf16[1,128,1024]{2,1,0:T(8,128)(2,1)S(1)}, bf16[1,128,1024]{2,1,0:T(8,128)(2,1)S(1)}, u32[]{:S(2)}, u32[]{:S(2)}) collective-permute-start(bf16[1,128,1024]{2,1,0:T(8,128)(2,1)S(1)} %get-tuple-element.18), channel_id=1, source_target_pairs={{0,1},{1,2},{2,3},{3,4},{4,5},{5,6},{6,7},{7,8},{8,9},{9,10},{10,1... | collective-permute-start | bytes 786440 | tf_op jit(solution)/shard_map/ppermute | solution.py:18
  10.1 5.1 %collective-permute-start.1 = (bf16[1,128,1024]{2,1,0:T(8,128)(2,1)S(1)}, bf16[1,128,1024]{2,1,0:T(8,128)(2,1)S(1)}, u32[]{:S(2)}, u32[]{:S(2)}) collective-permute-start(bf16[1,128,1024]{2,1,0:T(8,128)(2,1)S(1)} %get-tuple-element.19), channel_id=1, source_target_pairs={{1,0},{2,1},{3,2},{4,3},{5,4},{6,5},{7,6},{8,7},{9,8},{10,9},{11,1... | collective-permute-start | bytes 786440 | tf_op jit(solution)/shard_map/ppermute | solution.py:19
  26.8 0.7 copy-start.6
  27.2 0.9 copy-start.4
  27.5 1.8 copy-start.7
  28.1 53.4 %copy-start.8 = (f32[512]{0:T(512)S(1)}, f32[512]{0:T(512)}, u32[]{:S(2)}) copy-start(f32[512]{0:T(512)} %param.18) | copy-start | bytes 6148
  28.1 53.4 %copy-start.9 = (f32[100]{0:T(128)S(1)}, f32[100]{0:T(128)}, u32[]{:S(2)}) copy-start(f32[100]{0:T(128)} %param.19) | copy-start | bytes 1204
  29.3 339.3 %all-reduce.3.cloned.1.call-start = ((), (), s32[]{:S(2)}) async-start(), calls=%async_computation | async-start | bytes 851968 | tf_op jit(solution)/shard_map/psum | solution.py:100
  79.0 2.5 copy-start.3
  79.0 2.5 copy-start.5
  85.2 7.5 %copy-start.1 = (f32[512,1024]{1,0:T(8,128)S(1)}, f32[512,1024]{1,0:T(8,128)}, u32[]{:S(2)}) copy-start(f32[512,1024]{1,0:T(8,128)} %subtract_multiply_fusion) | copy-start | bytes 6291460
  109.9 86.4 %copy-start.2 = (f32[512,1024]{1,0:T(8,128)S(1)}, f32[512,1024]{1,0:T(8,128)}, u32[]{:S(2)}) copy-start(f32[512,1024]{1,0:T(8,128)} %scatter_custom_fusion.2) | copy-start | bytes 6291460
  110.8 85.6 %collective-permute-start.2 = (bf16[128,1024]{1,0:T(8,128)(2,1)}, bf16[128,1024]{1,0:T(8,128)(2,1)}, u32[]{:S(2)}, u32[]{:S(2)}) collective-permute-start(bf16[128,1024]{1,0:T(8,128)(2,1)} %get-tuple-element.16), channel_id=1, source_target_pairs={{0,1},{1,2},{2,3},{3,4},{4,5},{5,6},{6,7},{7,8},{8,9},{9,10},{10,1... | collective-permute-start | bytes 786440 | tf_op jit(solution)/shard_map/ppermute | solution.py:27
  112.7 83.6 %collective-permute-start.3 = (bf16[128,1024]{1,0:T(8,128)(2,1)}, bf16[128,1024]{1,0:T(8,128)(2,1)}, u32[]{:S(2)}, u32[]{:S(2)}) collective-permute-start(bf16[128,1024]{1,0:T(8,128)(2,1)} %get-tuple-element.17), channel_id=1, source_target_pairs={{1,0},{2,1},{3,2},{4,3},{5,4},{6,5},{7,6},{8,7},{9,8},{10,9},{11,1... | collective-permute-start | bytes 786440 | tf_op jit(solution)/shard_map/ppermute | solution.py:27
Sparse Core Ops, SparseCore 0:
  29.4 49.5 all-gather.3
  115.2 253.2 all-reduce.2
where the time goes:
time: 379 us; the launch traced here: 378 us
  waiting for transfers between devices  221 us (58%)
  blocking collectives  79.3 us (21%)
  other arithmetic  38 us (10%)
  between operations  17.4 us (5%)
  local copies, waits for them, and re-layouts  12.8 us (3%)
  starting transfers between devices  6.4 us (2%)
    psum x1, waiting for transfers between devices, per_device(): sums = lax.psum((wout_part, gain_part, local_loss), ('member', 'grid'))  170 us
    psum x1, blocking collectives, per_device(): sums = lax.psum((wout_part, gain_part, local_loss), ('member', 'grid'))  79.3 us
    all_gather x1, waiting for transfers between devices, per_device(): lax.all_gather(predicted_field[None], 'member', axis=0, tiled=True)  49.7 us
    scatter-add x3, other arithmetic, per_device(): collect.at[neighbours[slot]].add(weight_arrays[slot][:, None] * mixed_grad)  22.9 us
    gather x3, local copies, waits for them, and re-layouts, per_device(): jnp.take(extended, neighbours[slot], axis=0).astype(jnp.float32)  7.64 us
  transfers between devices with their start and end apart: 6, of which 3 were waited for; matrix products, arithmetic and copies ran while one was open for 1% of the time, Pallas kernels for 0%

commit v1 on v0

--- a/solution.py
+++ b/solution.py
@@ -97,7 +97,7 @@
         jnp.float32
     )
     owned = collect[rim : rim + mesh_count] + jnp.concatenate([from_below, from_above], axis=0)
-    sums = lax.psum((wout_part, gain_part, local_loss), ("member", "grid"))
+    sums = lax.psum(lax.psum((wout_part, gain_part, local_loss), "grid"), "member")
     fair_crps = sums[2] / (points * lax.axis_size("grid") * variables)
     return (fair_crps, owned[None].astype(jnp.bfloat16), sums[0], sums[1])
 

time: 379 us -> 447 us (1.18)
  waiting for transfers between devices: 221 us -> 279 us
  blocking collectives: 79.3 us -> 88.6 us
    psum x1 -> x2, waiting for transfers between devices: 170 us -> 228 us  [the longest x1 228 us: per_device(): lax.psum((wout_part, gain_part, local_loss), 'grid')]
    psum x1 -> x2, blocking collectives: 79.3 us -> 88.6 us  [the longest x1 67.9 us: per_device(): lax.psum((wout_part, gain_part, local_loss), 'grid')]
  transfers between devices with their start and end apart: 6 -> 7, of which waited for: 3 -> 3; matrix products, arithmetic and copies ran while one was open for 1% -> 7% of each run, Pallas kernels for 0% -> 0%
where the time goes in v1:
time: 447 us; the launch traced here: 446 us
  waiting for transfers between devices  279 us (62%)
  blocking collectives  88.6 us (20%)
  other arithmetic  38.7 us (9%)
  between operations  17.1 us (4%)
  local copies, waits for them, and re-layouts  12 us (3%)
  starting transfers between devices  5.95 us (1%)
    psum x1, waiting for transfers between devices, per_device(): lax.psum((wout_part, gain_part, local_loss), 'grid')  228 us
    psum x1, blocking collectives, per_device(): lax.psum((wout_part, gain_part, local_loss), 'grid')  67.9 us
    all_gather x1, waiting for transfers between devices, per_device(): lax.all_gather(predicted_field[None], 'member', axis=0, tiled=True)  49.6 us
    scatter-add x3, other arithmetic, per_device(): collect.at[neighbours[slot]].add(weight_arrays[slot][:, None] * mixed_grad)  23 us
    psum x1, blocking collectives, per_device(): lax.psum(lax.psum((wout_part, gain_part, local_loss), 'grid'), 'member')  20.7 us
  transfers between devices with their start and end apart: 7, of which 3 were waited for; matrix products, arithmetic and copies ran while one was open for 7% of the time, Pallas kernels for 0%

profile of v1, /device:TPU:2, one launch (start us, length us, event | category | flops | bytes accessed | tf_op | source)
XLA Modules:
  0.0 445.9 jit_solution(17256275730440772165)
XLA Ops:
  7.2 0.0 copy-start
  7.2 0.0 all-gather.4.cloned.1.call-start
  7.2 1.1 fusion.24
  8.3 1.8 collective-permute-start
  10.1 1.3 collective-permute-start.1
  11.4 0.8 fusion.26
  12.3 0.7 reduce_sum.90
  13.0 0.7 broadcast_divide_fusion
  13.8 0.0 collective-permute-done
  13.8 1.5 collective-permute-done.1
  15.2 1.1 maximum_bitcast_fusion
  16.3 2.1 gather_fusion.2
  18.4 2.8 gather_fusion.1
  21.2 2.8 gather_fusion
  24.0 2.8 fusion.21
  26.8 0.0 copy-start.6
  26.8 0.3 multiply_reduce_fusion.2
  27.2 0.3 copy-done.6
  27.5 0.3 multiply_convert_fusion
  27.8 0.0 copy-done
  27.9 0.3 copy-done.4
  28.1 1.1 fusion.11
  29.3 0.0 all-gather.4.cloned.1.call-update
  29.3 0.0 all-reduce.5.cloned.1.call-start
  29.4 0.0 copy-done.7
  29.4 49.6 %all-gather.4.cloned.1.call-done = f32[8,100,512]{2,1,0:T(8,128)} async-done(((f32[1,100,512]{2,1,0:T(8,128)}), f32[8,100,512]{2,1,0:T(8,128)}) %all-gather.4.cloned.1.call-update) | async-done | bytes 1638416 | tf_op jit(solution)/shard_map/all_gather | solution.py:71
  79.0 2.5 fusion.10
  81.5 0.0 copy-done.8
  81.6 0.8 fusion.19
  82.4 1.1 fusion.27
  83.4 2.1 multiply_reduce_fusion
  85.5 0.0 all-reduce.5.cloned.1.call-update
  85.6 0.2 all-reduce.7.cloned.1.call-start
  85.8 3.5 subtract_multiply_fusion
  89.3 7.4 %scatter_custom_fusion = f32[512,1024]{1,0:T(8,128)} fusion(s32[512]{0:T(512)S(1)} %bitcast.51, f32[512,1024]{1,0:T(8,128)} %subtract_multiply_fusion, f32[]{:T(128)} %constant.19.clone.1, f32[512]{0:T(512)S(1)} %bitcast.42), kind=kCustom, calls=%fused_computation.14 | custom fusion | flops 1048576 | bytes 4196356 | tf_op jit(solution)/shard_map/scatter-add | solution.py:94
  96.7 7.8 %scatter_custom_fusion.1 = f32[512,1024]{1,0:T(8,128)} fusion(f32[512,1024]{1,0:T(8,128)} %scatter_custom_fusion, s32[512]{0:T(512)S(1)} %bitcast.50, f32[512,1024]{1,0:T(8,128)S(1)} %copy-done.1, f32[512]{0:T(512)S(1)} %bitcast.40), kind=kCustom, calls=%fused_computation.12 | custom fusion | flops 1048576 | bytes 4196352 | tf_op jit(solution)/shard_map/scatter-add | solution.py:94
  104.5 7.8 %scatter_custom_fusion.2 = f32[512,1024]{1,0:T(8,128)} fusion(f32[512,1024]{1,0:T(8,128)} %scatter_custom_fusion.1, s32[512]{0:T(512)S(1)} %bitcast.49, f32[512,1024]{1,0:T(8,128)S(1)} %copy-done.1, f32[512]{0:T(512)S(1)} %bitcast.38), kind=kCustom, calls=%fused_computation.10 | custom fusion | flops 1048576 | bytes 4196352 | tf_op jit(solution)/shard_map/scatter-add | solution.py:94
  112.3 1.9 convert.6
  114.2 1.3 collective-permute-start.2
  115.5 1.3 collective-permute-start.3
  116.8 228.0 %all-reduce.5.cloned.1.call-done = f32[100,1024]{1,0:T(8,128)} async-done(((f32[100,1024]{1,0:T(8,128)}), f32[100,1024]{1,0:T(8,128)}) %all-reduce.5.cloned.1.call-update) | async-done | bytes 409616 | tf_op jit(solution)/shard_map/psum | solution.py:100
  344.9 0.0 all-reduce.7.cloned.1.call-update
  346.2 67.9 %all-reduce = (f32[]{:T(128)}, f32[1024]{0:T(1024)S(1)}) all-reduce(f32[]{:T(128)S(6)} %sub.46, f32[1024]{0:T(1024)S(1)} %get-tuple-element.5), channel_id=1, replica_groups=mesh['member'=8,'grid'=32] {'grid'}, use_global_device_ids=true, to_apply=%region_6.8 | all-reduce | flops 1025 | bytes 8200 | tf_op jit(solution)/shard_map/psum | solution.py:100
  414.1 20.7 %all-reduce.1 = (f32[]{:T(128)}, f32[1024]{0:T(1024)}) all-reduce(f32[]{:T(128)} %get-tuple-element.12, f32[1024]{0:T(1024)S(1)} %get-tuple-element.13), channel_id=1, replica_groups=mesh['member'=8,'grid'=32] {'member'}, use_global_device_ids=true, to_apply=%region_7.9 | all-reduce | flops 1025 | bytes 8200 | tf_op jit(solution)/shard_map/psum | solution.py:100
  435.4 0.0 collective-permute-done.2
  435.4 0.0 collective-permute-done.3
  435.5 0.9 fusion.17
  436.4 1.8 copy.20
  (29 shorter events, 0.1 us)
Async XLA Ops:
  7.2 20.7 %copy-start = (bf16[100,1024]{1,0:T(8,128)(2,1)S(1)}, bf16[100,1024]{1,0:T(8,128)(2,1)}, u32[]{:S(2)}) copy-start(bf16[100,1024]{1,0:T(8,128)(2,1)} %param.20) | copy-start | bytes 614404
  7.2 71.9 %all-gather.4.cloned.1.call-start = ((), (), s32[]{:S(2)}) async-start(), calls=%async_computation.2 | async-start | bytes 1916928 | tf_op jit(solution)/shard_map/all_gather | solution.py:71
  8.3 5.4 %collective-permute-start = (bf16[1,128,1024]{2,1,0:T(8,128)(2,1)S(1)}, bf16[1,128,1024]{2,1,0:T(8,128)(2,1)S(1)}, u32[]{:S(2)}, u32[]{:S(2)}) collective-permute-start(bf16[1,128,1024]{2,1,0:T(8,128)(2,1)S(1)} %get-tuple-element.20), channel_id=1, source_target_pairs={{0,1},{1,2},{2,3},{3,4},{4,5},{5,6},{6,7},{7,8},{8,9},{9,10},{10,1... | collective-permute-start | bytes 786440 | tf_op jit(solution)/shard_map/ppermute | solution.py:18
  10.1 5.1 %collective-permute-start.1 = (bf16[1,128,1024]{2,1,0:T(8,128)(2,1)S(1)}, bf16[1,128,1024]{2,1,0:T(8,128)(2,1)S(1)}, u32[]{:S(2)}, u32[]{:S(2)}) collective-permute-start(bf16[1,128,1024]{2,1,0:T(8,128)(2,1)S(1)} %get-tuple-element.21), channel_id=1, source_target_pairs={{1,0},{2,1},{3,2},{4,3},{5,4},{6,5},{7,6},{8,7},{9,8},{10,9},{11,1... | collective-permute-start | bytes 786440 | tf_op jit(solution)/shard_map/ppermute | solution.py:19
  26.8 0.7 copy-start.6
  27.2 0.9 copy-start.4
  27.5 1.8 copy-start.7
  28.1 53.4 %copy-start.8 = (f32[512]{0:T(512)S(1)}, f32[512]{0:T(512)}, u32[]{:S(2)}) copy-start(f32[512]{0:T(512)} %param.18) | copy-start | bytes 6148
  28.1 53.4 %copy-start.9 = (f32[100]{0:T(128)S(1)}, f32[100]{0:T(128)}, u32[]{:S(2)}) copy-start(f32[100]{0:T(128)} %param.19) | copy-start | bytes 1204
  29.3 315.6 %all-reduce.5.cloned.1.call-start = ((), (), s32[]{:S(2)}) async-start(), calls=%async_computation | async-start | bytes 851968 | tf_op jit(solution)/shard_map/psum | solution.py:100
  79.0 2.5 copy-start.3
  79.0 2.5 copy-start.5
  85.6 350.8 %all-reduce.7.cloned.1.call-start = ((), (), s32[]{:S(2)}) async-start(), calls=%async_computation.1 | async-start | bytes 851968 | tf_op jit(solution)/shard_map/psum | solution.py:100
  89.3 7.5 %copy-start.1 = (f32[512,1024]{1,0:T(8,128)S(1)}, f32[512,1024]{1,0:T(8,128)}, u32[]{:S(2)}) copy-start(f32[512,1024]{1,0:T(8,128)} %subtract_multiply_fusion) | copy-start | bytes 6291460
  112.3 323.2 %copy-start.2 = (f32[512,1024]{1,0:T(8,128)S(1)}, f32[512,1024]{1,0:T(8,128)}, u32[]{:S(2)}) copy-start(f32[512,1024]{1,0:T(8,128)} %scatter_custom_fusion.2) | copy-start | bytes 6291460
  114.2 321.2 %collective-permute-start.2 = (bf16[128,1024]{1,0:T(8,128)(2,1)S(1)}, bf16[128,1024]{1,0:T(8,128)(2,1)S(1)}, u32[]{:S(2)}, u32[]{:S(2)}) collective-permute-start(bf16[128,1024]{1,0:T(8,128)(2,1)S(1)} %get-tuple-element.18), channel_id=1, source_target_pairs={{0,1},{1,2},{2,3},{3,4},{4,5},{5,6},{6,7},{7,8},{8,9},{9,10},{10,1... | collective-permute-start | bytes 786440 | tf_op jit(solution)/shard_map/ppermute | solution.py:27
  115.5 319.9 %collective-permute-start.3 = (bf16[128,1024]{1,0:T(8,128)(2,1)S(1)}, bf16[128,1024]{1,0:T(8,128)(2,1)S(1)}, u32[]{:S(2)}, u32[]{:S(2)}) collective-permute-start(bf16[128,1024]{1,0:T(8,128)(2,1)S(1)} %get-tuple-element.19), channel_id=1, source_target_pairs={{1,0},{2,1},{3,2},{4,3},{5,4},{6,5},{7,6},{8,7},{9,8},{10,9},{11,1... | collective-permute-start | bytes 786440 | tf_op jit(solution)/shard_map/ppermute | solution.py:27
Sparse Core Ops, SparseCore 0:
  29.4 49.5 all-gather.3
  85.7 259.1 all-reduce.4
  347.7 72.8 all-reduce.6
